TPU v7x, 256 devices: a whole 4x4x8 slice. The times are simulated.
256 devices in a mesh: outer: 8 (over x, y_lo), inner: 32 (over y_hi, z, core).
Axes of the slice: x: 4, y: 4 (y_hi: 2, y_lo: 2; y = y_hi * 2 + y_lo), z: 8, core: 2. Of those that a mesh axis runs over, the one named last changes fastest.
Arguments:
- queries: bfloat16 [131072, 1024], P(('outer', 'inner')), may hold values from -6 to 6
- keys: bfloat16 [131072, 128], P(('outer', 'inner')), may hold values from -6 to 6
- values: bfloat16 [131072, 128], P(('outer', 'inner')), may hold values from -6 to 6
- grad_out: bfloat16 [131072, 1024], P(('outer', 'inner')), may hold values from -6 to 6
- turn_ids: int32 [131072], P(('outer', 'inner')), may hold values from 0 to 255, never falling along the last dimension, each value on 1 to 2048 neighbouring positions
- tool_spans: int32 [128, 2], replicated, may hold values from 0 to 131072, as said below
Outputs:
- grad_queries: bfloat16 [131072, 1024], P(('outer', 'inner'))
- grad_keys: bfloat16 [131072, 128], P(('outer', 'inner'))
- grad_values: bfloat16 [131072, 128], P(('outer', 'inner'))
Inputs may be any that keep to these rules, and one draw needn't show every extreme that they name: `tool_spans`: rows are sorted and disjoint; each span has at least one position.
All inputs are finite; a program needn't handle non-finite values.
Results may differ from a plain program's by a relative error of at most 0.025.
Values may be sent and summed in bfloat16 or wider, within the bound.
A program may use at most 64 MiB of HBM per device.

v0:
```python
import jax
import jax.numpy as jnp
from jax import lax
from jax.sharding import PartitionSpec as P


def from_behind(block, axis, distance):
    devices = range(lax.axis_size(axis))
    route = [(i - distance, i) for i in devices if i - distance in devices]
    return lax.ppermute(block, axis, route)


def on_device(queries, keys, values, grad_out, turn_ids, tool_spans):
    row_count = keys.shape[0]
    head_width = keys.shape[1]
    head_count = queries.shape[1] // head_width
    reach = 4 * row_count
    score_scale = head_width ** (-0.5)
    inner_count = lax.axis_size("inner")
    inner_pos = lax.axis_index("inner")
    block_index = lax.axis_index("outer") * inner_count + inner_pos
    arrived = []
    held = (keys, values, turn_ids)
    for hops in range(4):
        held = from_behind((held[0], held[1], held[2]), ("outer", "inner"), 1)
        arrived.append(held)
    key_window = jnp.concatenate(
        [arrived[3][0], arrived[2][0], arrived[1][0], arrived[0][0], keys], axis=0
    )
    value_window = jnp.concatenate(
        [arrived[3][1], arrived[2][1], arrived[1][1], arrived[0][1], values], axis=0
    )
    turn_key = jnp.concatenate(
        [arrived[3][2], arrived[2][2], arrived[1][2], arrived[0][2], turn_ids], axis=0
    )
    key_pos = (block_index - 4) * row_count + jnp.arange(5 * row_count, dtype=jnp.int32)
    tool_key = jnp.any(
        (key_pos[:, None] >= tool_spans[None, :, 0]) & (key_pos[:, None] < tool_spans[None, :, 1]),
        axis=1,
    )
    open_key = jnp.logical_not(tool_key)
    query_pos = block_index * row_count + jnp.arange(row_count, dtype=jnp.int32)
    merged = row_count * head_count
    step_rows = min(512, merged)
    step_count = merged // step_rows
    query_parts = queries.reshape(step_count, step_rows, head_width)
    cotangent_parts = grad_out.reshape(step_count, step_rows, head_width)
    pos_parts = jnp.repeat(query_pos, head_count).reshape(step_count, step_rows)
    turn_parts = jnp.repeat(turn_ids, head_count).reshape(step_count, step_rows)
    contract_rows = (((0,), (0,)), ((), ()))

    def tile_step(carry, parts):
        query_part, cotangent, pos_part, turn_part = parts
        distance = pos_part[:, None] - key_pos[None, :]
        visible = (key_pos[None, :] >= 0) & (distance >= 0) & (distance < reach)
        visible = visible & (open_key[None, :] | (turn_key[None, :] == turn_part[:, None]))
        scores = jnp.dot(query_part, key_window.T, preferred_element_type=jnp.float32) * score_scale
        masked = jnp.where(visible, scores, -jnp.inf)
        row_top = jnp.max(masked, axis=-1, keepdims=True)
        log_total = row_top + jnp.log(jnp.sum(jnp.exp(masked - row_top), axis=-1, keepdims=True))
        probs = jnp.exp(masked - log_total)
        probs_low = probs.astype(jnp.bfloat16)
        attended = jnp.dot(probs_low, value_window, preferred_element_type=jnp.float32).astype(
            jnp.bfloat16
        )
        delta = jnp.sum(cotangent.astype(jnp.float32) * attended.astype(jnp.float32), axis=-1)
        dprobs = jnp.dot(cotangent, value_window.T, preferred_element_type=jnp.float32)
        dscores = (probs * (dprobs - delta[:, None])).astype(jnp.bfloat16)
        grad_query = (
            jnp.dot(dscores, key_window, preferred_element_type=jnp.float32) * score_scale
        ).astype(jnp.bfloat16)
        grad_key_part = (
            lax.dot_general(dscores, query_part, contract_rows, preferred_element_type=jnp.float32)
            * score_scale
        )
        grad_value_part = lax.dot_general(
            probs_low, cotangent, contract_rows, preferred_element_type=jnp.float32
        )
        return ((carry[0] + grad_key_part, carry[1] + grad_value_part), grad_query)

    zeros_window = jnp.zeros((5 * row_count, head_width), jnp.float32)
    (grad_key_window, grad_value_window), grad_query_parts = lax.scan(
        tile_step,
        (zeros_window, zeros_window),
        (query_parts, cotangent_parts, pos_parts, turn_parts),
    )
    grad_queries = grad_query_parts.reshape(row_count, head_count * head_width)

    def piece(hops):
        lower = (4 - hops) * row_count
        return (
            grad_key_window[lower : lower + row_count],
            grad_value_window[lower : lower + row_count],
        )

    running = piece(4)
    for hops in (3, 2, 1, 0):
        moved = from_behind((running[0], running[1]), ("outer", "inner"), -1)
        local_part = piece(hops)
        running = (moved[0] + local_part[0], moved[1] + local_part[1])
    key_total, value_total = running
    return (grad_queries, key_total.astype(jnp.bfloat16), value_total.astype(jnp.bfloat16))


def solution(mesh):
    placed = (
        P(("outer", "inner"), None),
        P(("outer", "inner"), None),
        P(("outer", "inner"), None),
        P(("outer", "inner"), None),
        P(("outer", "inner")),
        P(),
    )
    return jax.shard_map(
        on_device,
        mesh=mesh,
        in_specs=placed,
        out_specs=(
            P(("outer", "inner"), None),
            P(("outer", "inner"), None),
            P(("outer", "inner"), None),
        ),
        check_vma=False,
    )
```

profile of v0, /device:TPU:6, one launch (start us, length us, event | category | flops | bytes accessed | tf_op | source)
XLA Modules:
  0.0 295.7 jit_solution(16660408079161414719)
XLA Ops:
  9.2 6.7 %collective-permute-done = s32[512]{0:T(512)S(1)} collective-permute-done((s32[512]{0:T(512)}, s32[512]{0:T(512)S(1)}, u32[]{:S(2)}, u32[]{:S(2)}) %collective-permute-start) | collective-permute-done | bytes 2080 | tf_op jit(solution)/shard_map/ppermute | solution.py:10
  17.8 7.2 %collective-permute-done.1 = s32[512]{0:T(512)S(1)} collective-permute-done((s32[512]{0:T(512)S(1)}, s32[512]{0:T(512)S(1)}, u32[]{:S(2)}, u32[]{:S(2)}) %collective-permute-start.1) | collective-permute-done | bytes 2080 | tf_op jit(solution)/shard_map/ppermute | solution.py:10
  28.5 5.7 %collective-permute-done.2 = s32[512]{0:T(512)} collective-permute-done((s32[512]{0:T(512)S(1)}, s32[512]{0:T(512)}, u32[]{:S(2)}, u32[]{:S(2)}) %collective-permute-start.2) | collective-permute-done | bytes 2080 | tf_op jit(solution)/shard_map/ppermute | solution.py:10
  54.4 4.0 %collective-permute-done.9 = bf16[512,128]{1,0:T(8,128)(2,1)S(1)} collective-permute-done((bf16[512,128]{1,0:T(8,128)(2,1)S(1)}, bf16[512,128]{1,0:T(8,128)(2,1)S(1)}, u32[]{:S(2)}, u32[]{:S(2)}) %collective-permute-start.9) | collective-permute-done | bytes 131104 | tf_op jit(solution)/shard_map/ppermute | solution.py:10
  64.9 4.1 %collective-permute-done.10 = bf16[512,128]{1,0:T(8,128)(2,1)S(1)} collective-permute-done((bf16[512,128]{1,0:T(8,128)(2,1)S(1)}, bf16[512,128]{1,0:T(8,128)(2,1)S(1)}, u32[]{:S(2)}, u32[]{:S(2)}) %collective-permute-start.10) | collective-permute-done | bytes 131104 | tf_op jit(solution)/shard_map/ppermute | solution.py:10
  71.0 8.4 %collective-permute-done.11 = bf16[512,128]{1,0:T(8,128)(2,1)S(1)} collective-permute-done((bf16[512,128]{1,0:T(8,128)(2,1)S(1)}, bf16[512,128]{1,0:T(8,128)(2,1)S(1)}, u32[]{:S(2)}, u32[]{:S(2)}) %collective-permute-start.11) | collective-permute-done | bytes 131104 | tf_op jit(solution)/shard_map/ppermute | solution.py:10
  79.6 170.0 %while.15 = (s32[]{:T(128)}, f32[2560,128]{1,0:T(8,128)S(1)}, f32[2560,128]{1,0:T(8,128)S(1)}, bf16[8,512,128]{2,1,0:T(8,128)(2,1)}, s32[8,512]{1,0:T(8,128)S(1)...) while((s32[]{:T(128)}, f32[2560,128]{1,0:T(8,128)S(1)}, ...), condition=%wide.region_5.6_spmd.clone, body=%wide.region_1.5_spmd.clone.sunk | while | flops 2042894848 | bytes 88026936 | solution.py:82
  80.4 3.9 %fusion.56 = (f32[512]{0:T(512)S(1)}, f32[512,2560]{1,0:T(8,128)S(1)}) fusion(bf16[2560,128]{1,0:T(8,128)(2,1)} %get-tuple-element.304, bf16[8,512,128]{2,1,0:T(8,128)(2,1)} %get-tuple-element.303, s32[]{:T(128)} %get-tuple-element.280, s32[512]{0:T(512)S(1)} %bitcast.59, s32[2560]{0:T(1024)} %get-tuple-element.301, ...), kind=kOutput, calls=%fused_computation.64.clone.1 | convolution fusion | flops 349961728 | bytes 6064128 | tf_op jit(solution)/shard_map/while/body/eval_jaxpr/dot_general | solution.py:57
  87.6 4.0 %convolution_add_fusion.2 = f32[2560,128]{1,0:T(8,128)S(1)} fusion(f32[2560,128]{1,0:T(8,128)S(1)} %get-tuple-element.282, pred[]{:T(512)S(6)} %compare.3, bf16[1,512,128]{2,1,0:T(8,128)(2,1)S(1)} %constant_dynamic-slice_fusion.6, f32[512,2560]{1,0:T(8,128)} %copy-done, f32[512]{0:T(512)S(1)} %log_add_fusion.2), kind=kOutput, calls=%fused_computation.11.clone.1 | convolution fusion | flops 338821120 | bytes 7997441 | tf_op jit(solution)/shard_map/while/body/eval_jaxpr/dot_general | solution.py:76
  101.6 4.0 %fusion.56 = (f32[512]{0:T(512)S(1)}, f32[512,2560]{1,0:T(8,128)S(1)}) fusion(bf16[2560,128]{1,0:T(8,128)(2,1)} %get-tuple-element.304, bf16[8,512,128]{2,1,0:T(8,128)(2,1)} %get-tuple-element.303, s32[]{:T(128)} %get-tuple-element.280, s32[512]{0:T(512)S(1)} %bitcast.59, s32[2560]{0:T(1024)} %get-tuple-element.301, ...), kind=kOutput, calls=%fused_computation.64.clone.1 | convolution fusion | flops 349961728 | bytes 6064128 | tf_op jit(solution)/shard_map/while/body/eval_jaxpr/dot_general | solution.py:57
  108.8 4.0 %convolution_add_fusion.2 = f32[2560,128]{1,0:T(8,128)S(1)} fusion(f32[2560,128]{1,0:T(8,128)S(1)} %get-tuple-element.282, pred[]{:T(512)S(6)} %compare.3, bf16[1,512,128]{2,1,0:T(8,128)(2,1)S(1)} %constant_dynamic-slice_fusion.6, f32[512,2560]{1,0:T(8,128)} %copy-done, f32[512]{0:T(512)S(1)} %log_add_fusion.2), kind=kOutput, calls=%fused_computation.11.clone.1 | convolution fusion | flops 338821120 | bytes 7997441 | tf_op jit(solution)/shard_map/while/body/eval_jaxpr/dot_general | solution.py:76
  122.9 3.9 %fusion.56 = (f32[512]{0:T(512)S(1)}, f32[512,2560]{1,0:T(8,128)S(1)}) fusion(bf16[2560,128]{1,0:T(8,128)(2,1)} %get-tuple-element.304, bf16[8,512,128]{2,1,0:T(8,128)(2,1)} %get-tuple-element.303, s32[]{:T(128)} %get-tuple-element.280, s32[512]{0:T(512)S(1)} %bitcast.59, s32[2560]{0:T(1024)} %get-tuple-element.301, ...), kind=kOutput, calls=%fused_computation.64.clone.1 | convolution fusion | flops 349961728 | bytes 6064128 | tf_op jit(solution)/shard_map/while/body/eval_jaxpr/dot_general | solution.py:57
  130.1 4.0 %convolution_add_fusion.2 = f32[2560,128]{1,0:T(8,128)S(1)} fusion(f32[2560,128]{1,0:T(8,128)S(1)} %get-tuple-element.282, pred[]{:T(512)S(6)} %compare.3, bf16[1,512,128]{2,1,0:T(8,128)(2,1)S(1)} %constant_dynamic-slice_fusion.6, f32[512,2560]{1,0:T(8,128)} %copy-done, f32[512]{0:T(512)S(1)} %log_add_fusion.2), kind=kOutput, calls=%fused_computation.11.clone.1 | convolution fusion | flops 338821120 | bytes 7997441 | tf_op jit(solution)/shard_map/while/body/eval_jaxpr/dot_general | solution.py:76
  151.3 4.0 %convolution_add_fusion.2 = f32[2560,128]{1,0:T(8,128)S(1)} fusion(f32[2560,128]{1,0:T(8,128)S(1)} %get-tuple-element.282, pred[]{:T(512)S(6)} %compare.3, bf16[1,512,128]{2,1,0:T(8,128)(2,1)S(1)} %constant_dynamic-slice_fusion.6, f32[512,2560]{1,0:T(8,128)} %copy-done, f32[512]{0:T(512)S(1)} %log_add_fusion.2), kind=kOutput, calls=%fused_computation.11.clone.1 | convolution fusion | flops 338821120 | bytes 7997441 | tf_op jit(solution)/shard_map/while/body/eval_jaxpr/dot_general | solution.py:76
  165.4 3.9 %fusion.56 = (f32[512]{0:T(512)S(1)}, f32[512,2560]{1,0:T(8,128)S(1)}) fusion(bf16[2560,128]{1,0:T(8,128)(2,1)} %get-tuple-element.304, bf16[8,512,128]{2,1,0:T(8,128)(2,1)} %get-tuple-element.303, s32[]{:T(128)} %get-tuple-element.280, s32[512]{0:T(512)S(1)} %bitcast.59, s32[2560]{0:T(1024)} %get-tuple-element.301, ...), kind=kOutput, calls=%fused_computation.64.clone.1 | convolution fusion | flops 349961728 | bytes 6064128 | tf_op jit(solution)/shard_map/while/body/eval_jaxpr/dot_general | solution.py:57
  172.6 4.0 %convolution_add_fusion.2 = f32[2560,128]{1,0:T(8,128)S(1)} fusion(f32[2560,128]{1,0:T(8,128)S(1)} %get-tuple-element.282, pred[]{:T(512)S(6)} %compare.3, bf16[1,512,128]{2,1,0:T(8,128)(2,1)S(1)} %constant_dynamic-slice_fusion.6, f32[512,2560]{1,0:T(8,128)} %copy-done, f32[512]{0:T(512)S(1)} %log_add_fusion.2), kind=kOutput, calls=%fused_computation.11.clone.1 | convolution fusion | flops 338821120 | bytes 7997441 | tf_op jit(solution)/shard_map/while/body/eval_jaxpr/dot_general | solution.py:76
  193.8 4.0 %convolution_add_fusion.2 = f32[2560,128]{1,0:T(8,128)S(1)} fusion(f32[2560,128]{1,0:T(8,128)S(1)} %get-tuple-element.282, pred[]{:T(512)S(6)} %compare.3, bf16[1,512,128]{2,1,0:T(8,128)(2,1)S(1)} %constant_dynamic-slice_fusion.6, f32[512,2560]{1,0:T(8,128)} %copy-done, f32[512]{0:T(512)S(1)} %log_add_fusion.2), kind=kOutput, calls=%fused_computation.11.clone.1 | convolution fusion | flops 338821120 | bytes 7997441 | tf_op jit(solution)/shard_map/while/body/eval_jaxpr/dot_general | solution.py:76
  207.9 3.9 %fusion.56 = (f32[512]{0:T(512)S(1)}, f32[512,2560]{1,0:T(8,128)S(1)}) fusion(bf16[2560,128]{1,0:T(8,128)(2,1)} %get-tuple-element.304, bf16[8,512,128]{2,1,0:T(8,128)(2,1)} %get-tuple-element.303, s32[]{:T(128)} %get-tuple-element.280, s32[512]{0:T(512)S(1)} %bitcast.59, s32[2560]{0:T(1024)} %get-tuple-element.301, ...), kind=kOutput, calls=%fused_computation.64.clone.1 | convolution fusion | flops 349961728 | bytes 6064128 | tf_op jit(solution)/shard_map/while/body/eval_jaxpr/dot_general | solution.py:57
  215.1 4.0 %convolution_add_fusion.2 = f32[2560,128]{1,0:T(8,128)S(1)} fusion(f32[2560,128]{1,0:T(8,128)S(1)} %get-tuple-element.282, pred[]{:T(512)S(6)} %compare.3, bf16[1,512,128]{2,1,0:T(8,128)(2,1)S(1)} %constant_dynamic-slice_fusion.6, f32[512,2560]{1,0:T(8,128)} %copy-done, f32[512]{0:T(512)S(1)} %log_add_fusion.2), kind=kOutput, calls=%fused_computation.11.clone.1 | convolution fusion | flops 338821120 | bytes 7997441 | tf_op jit(solution)/shard_map/while/body/eval_jaxpr/dot_general | solution.py:76
  229.1 3.9 %fusion.56 = (f32[512]{0:T(512)S(1)}, f32[512,2560]{1,0:T(8,128)S(1)}) fusion(bf16[2560,128]{1,0:T(8,128)(2,1)} %get-tuple-element.304, bf16[8,512,128]{2,1,0:T(8,128)(2,1)} %get-tuple-element.303, s32[]{:T(128)} %get-tuple-element.280, s32[512]{0:T(512)S(1)} %bitcast.59, s32[2560]{0:T(1024)} %get-tuple-element.301, ...), kind=kOutput, calls=%fused_computation.64.clone.1 | convolution fusion | flops 349961728 | bytes 6064128 | tf_op jit(solution)/shard_map/while/body/eval_jaxpr/dot_general | solution.py:57
  236.3 4.0 %convolution_add_fusion.2 = f32[2560,128]{1,0:T(8,128)S(1)} fusion(f32[2560,128]{1,0:T(8,128)S(1)} %get-tuple-element.282, pred[]{:T(512)S(6)} %compare.3, bf16[1,512,128]{2,1,0:T(8,128)(2,1)S(1)} %constant_dynamic-slice_fusion.6, f32[512,2560]{1,0:T(8,128)} %copy-done, f32[512]{0:T(512)S(1)} %log_add_fusion.2), kind=kOutput, calls=%fused_computation.11.clone.1 | convolution fusion | flops 338821120 | bytes 7997441 | tf_op jit(solution)/shard_map/while/body/eval_jaxpr/dot_general | solution.py:76
  255.5 8.0 %collective-permute-start.17 = (f32[512,128]{1,0:T(8,128)S(1)}, f32[512,128]{1,0:T(8,128)S(1)}, u32[]{:S(2)}, u32[]{:S(2)}) collective-permute-start(f32[512,128]{1,0:T(8,128)S(1)} %slice_add_fusion.2), channel_id=1, source_target_pairs={{1,0},{2,1},{3,2},{4,3},{5,4},{6,5},{7,6},{8,7},{9,8},{10,9},{11,1... | collective-permute-start | bytes 786440 | tf_op jit(solution)/shard_map/ppermute | solution.py:10
  267.4 8.0 %collective-permute-start.18 = (f32[512,128]{1,0:T(8,128)S(1)}, f32[512,128]{1,0:T(8,128)S(1)}, u32[]{:S(2)}, u32[]{:S(2)}) collective-permute-start(f32[512,128]{1,0:T(8,128)S(1)} %slice_add_fusion.1), channel_id=1, source_target_pairs={{1,0},{2,1},{3,2},{4,3},{5,4},{6,5},{7,6},{8,7},{9,8},{10,9},{11,1... | collective-permute-start | bytes 786440 | tf_op jit(solution)/shard_map/ppermute | solution.py:10
  279.4 8.0 %collective-permute-start.19 = (f32[512,128]{1,0:T(8,128)S(1)}, f32[512,128]{1,0:T(8,128)S(1)}, u32[]{:S(2)}, u32[]{:S(2)}) collective-permute-start(f32[512,128]{1,0:T(8,128)S(1)} %slice_add_fusion), channel_id=1, source_target_pairs={{1,0},{2,1},{3,2},{4,3},{5,4},{6,5},{7,6},{8,7},{9,8},{10,9},{11,1... | collective-permute-start | bytes 786440 | tf_op jit(solution)/shard_map/ppermute | solution.py:10
  (253 shorter events, 177.9 us)
Async XLA Ops:
  0.6 35.5 %collective-permute-start.4 = (bf16[512,128]{1,0:T(8,128)(2,1)}, bf16[512,128]{1,0:T(8,128)(2,1)S(1)}, u32[]{:S(2)}, u32[]{:S(2)}) collective-permute-start(bf16[512,128]{1,0:T(8,128)(2,1)} %param.9), channel_id=1, source_target_pairs={{0,1},{1,2},{2,3},{3,4},{4,5},{5,6},{6,7},{7,8},{8,9},{9,10},{10,1... | collective-permute-start | bytes 393224 | tf_op jit(solution)/shard_map/ppermute | solution.py:10
  2.6 45.4 %collective-permute-start.8 = (bf16[512,128]{1,0:T(8,128)(2,1)}, bf16[512,128]{1,0:T(8,128)(2,1)S(1)}, u32[]{:S(2)}, u32[]{:S(2)}) collective-permute-start(bf16[512,128]{1,0:T(8,128)(2,1)} %param.10), channel_id=1, source_target_pairs={{0,1},{1,2},{2,3},{3,4},{4,5},{5,6},{6,7},{7,8},{8,9},{9,10},{10,1... | collective-permute-start | bytes 393224 | tf_op jit(solution)/shard_map/ppermute | solution.py:10
  6.5 9.4 %collective-permute-start = (s32[512]{0:T(512)}, s32[512]{0:T(512)S(1)}, u32[]{:S(2)}, u32[]{:S(2)}) collective-permute-start(s32[512]{0:T(512)} %param.12), channel_id=1, source_target_pairs={{0,1},{1,2},{2,3},{3,4},{4,5},{5,6},{6,7},{7,8},{8,9},{9,10},{10,1... | collective-permute-start | bytes 6152 | tf_op jit(solution)/shard_map/ppermute | solution.py:10
  15.9 20.3 %copy-start.8 = (s32[512]{0:T(512)}, s32[512]{0:T(512)S(1)}, u32[]{:S(2)}) copy-start(s32[512]{0:T(512)S(1)} %collective-permute-done) | copy-start | bytes 6148
  15.9 9.1 %collective-permute-start.1 = (s32[512]{0:T(512)S(1)}, s32[512]{0:T(512)S(1)}, u32[]{:S(2)}, u32[]{:S(2)}) collective-permute-start(s32[512]{0:T(512)S(1)} %collective-permute-done), channel_id=1, source_target_pairs={{0,1},{1,2},{2,3},{3,4},{4,5},{5,6},{6,7},{7,8},{8,9},{9,10},{10,1... | collective-permute-start | bytes 6152 | tf_op jit(solution)/shard_map/ppermute | solution.py:10
  25.0 15.2 %copy-start.9 = (s32[512]{0:T(512)}, s32[512]{0:T(512)S(1)}, u32[]{:S(2)}) copy-start(s32[512]{0:T(512)S(1)} %collective-permute-done.1) | copy-start | bytes 6148
  25.0 9.2 %collective-permute-start.2 = (s32[512]{0:T(512)S(1)}, s32[512]{0:T(512)}, u32[]{:S(2)}, u32[]{:S(2)}) collective-permute-start(s32[512]{0:T(512)S(1)} %collective-permute-done.1), channel_id=1, source_target_pairs={{0,1},{1,2},{2,3},{3,4},{4,5},{5,6},{6,7},{7,8},{8,9},{9,10},{10,1... | collective-permute-start | bytes 6152 | tf_op jit(solution)/shard_map/ppermute | solution.py:10
  34.2 12.4 %collective-permute-start.3 = (s32[512]{0:T(512)}, s32[512]{0:T(512)}, u32[]{:S(2)}, u32[]{:S(2)}) collective-permute-start(s32[512]{0:T(512)} %collective-permute-done.2), channel_id=1, source_target_pairs={{0,1},{1,2},{2,3},{3,4},{4,5},{5,6},{6,7},{7,8},{8,9},{9,10},{10,1... | collective-permute-start | bytes 6152 | tf_op jit(solution)/shard_map/ppermute | solution.py:10
  36.2 13.7 %collective-permute-start.5 = (bf16[512,128]{1,0:T(8,128)(2,1)S(1)}, bf16[512,128]{1,0:T(8,128)(2,1)S(1)}, u32[]{:S(2)}, u32[]{:S(2)}) collective-permute-start(bf16[512,128]{1,0:T(8,128)(2,1)S(1)} %collective-permute-done.4), channel_id=1, source_target_pairs={{0,1},{1,2},{2,3},{3,4},{4,5},{5,6},{6,7},{7,8},{8,9},{9,10},{10,1... | collective-permute-start | bytes 393224 | tf_op jit(solution)/shard_map/ppermute | solution.py:10
  40.4 30.6 %copy-start.2 = (bf16[512,128]{1,0:T(8,128)(2,1)S(1)}, bf16[512,128]{1,0:T(8,128)(2,1)}, u32[]{:S(2)}) copy-start(bf16[512,128]{1,0:T(8,128)(2,1)} %param.9) | copy-start | bytes 393220
  42.7 36.8 %copy-start.3 = (bf16[512,128]{1,0:T(8,128)(2,1)S(1)}, bf16[512,128]{1,0:T(8,128)(2,1)}, u32[]{:S(2)}) copy-start(bf16[512,128]{1,0:T(8,128)(2,1)} %param.10) | copy-start | bytes 393220
  48.0 10.5 %collective-permute-start.9 = (bf16[512,128]{1,0:T(8,128)(2,1)S(1)}, bf16[512,128]{1,0:T(8,128)(2,1)S(1)}, u32[]{:S(2)}, u32[]{:S(2)}) collective-permute-start(bf16[512,128]{1,0:T(8,128)(2,1)S(1)} %collective-permute-done.8), channel_id=1, source_target_pairs={{0,1},{1,2},{2,3},{3,4},{4,5},{5,6},{6,7},{7,8},{8,9},{9,10},{10,1... | collective-permute-start | bytes 393224 | tf_op jit(solution)/shard_map/ppermute | solution.py:10
  49.9 10.5 %collective-permute-start.6 = (bf16[512,128]{1,0:T(8,128)(2,1)S(1)}, bf16[512,128]{1,0:T(8,128)(2,1)S(1)}, u32[]{:S(2)}, u32[]{:S(2)}) collective-permute-start(bf16[512,128]{1,0:T(8,128)(2,1)S(1)} %collective-permute-done.5), channel_id=1, source_target_pairs={{0,1},{1,2},{2,3},{3,4},{4,5},{5,6},{6,7},{7,8},{8,9},{9,10},{10,1... | collective-permute-start | bytes 393224 | tf_op jit(solution)/shard_map/ppermute | solution.py:10
  58.5 10.5 %collective-permute-start.10 = (bf16[512,128]{1,0:T(8,128)(2,1)S(1)}, bf16[512,128]{1,0:T(8,128)(2,1)S(1)}, u32[]{:S(2)}, u32[]{:S(2)}) collective-permute-start(bf16[512,128]{1,0:T(8,128)(2,1)S(1)} %collective-permute-done.9), channel_id=1, source_target_pairs={{0,1},{1,2},{2,3},{3,4},{4,5},{5,6},{6,7},{7,8},{8,9},{9,10},{10,1... | collective-permute-start | bytes 393224 | tf_op jit(solution)/shard_map/ppermute | solution.py:10
  60.4 10.5 %collective-permute-start.7 = (bf16[512,128]{1,0:T(8,128)(2,1)S(1)}, bf16[512,128]{1,0:T(8,128)(2,1)S(1)}, u32[]{:S(2)}, u32[]{:S(2)}) collective-permute-start(bf16[512,128]{1,0:T(8,128)(2,1)S(1)} %collective-permute-done.6), channel_id=1, source_target_pairs={{0,1},{1,2},{2,3},{3,4},{4,5},{5,6},{6,7},{7,8},{8,9},{9,10},{10,1... | collective-permute-start | bytes 393224 | tf_op jit(solution)/shard_map/ppermute | solution.py:10
  69.0 10.5 %collective-permute-start.11 = (bf16[512,128]{1,0:T(8,128)(2,1)S(1)}, bf16[512,128]{1,0:T(8,128)(2,1)S(1)}, u32[]{:S(2)}, u32[]{:S(2)}) collective-permute-start(bf16[512,128]{1,0:T(8,128)(2,1)S(1)} %collective-permute-done.10), channel_id=1, source_target_pairs={{0,1},{1,2},{2,3},{3,4},{4,5},{5,6},{6,7},{7,8},{8,9},{9,10},{10,1... | collective-permute-start | bytes 393224 | tf_op jit(solution)/shard_map/ppermute | solution.py:10
  249.6 5.8 %collective-permute-start.16 = (f32[512,128]{1,0:T(8,128)S(1)}, f32[512,128]{1,0:T(8,128)S(1)}, u32[]{:S(2)}, u32[]{:S(2)}) collective-permute-start(f32[512,128]{1,0:T(8,128)S(1)} %slice.43), channel_id=1, source_target_pairs={{1,0},{2,1},{3,2},{4,3},{5,4},{6,5},{7,6},{8,7},{9,8},{10,9},{11,1... | collective-permute-start | bytes 786440 | tf_op jit(solution)/shard_map/ppermute | solution.py:10
  251.6 11.9 %collective-permute-start.12 = (f32[512,128]{1,0:T(8,128)S(1)}, f32[512,128]{1,0:T(8,128)S(1)}, u32[]{:S(2)}, u32[]{:S(2)}) collective-permute-start(f32[512,128]{1,0:T(8,128)S(1)} %slice.38), channel_id=1, source_target_pairs={{1,0},{2,1},{3,2},{4,3},{5,4},{6,5},{7,6},{8,7},{9,8},{10,9},{11,1... | collective-permute-start | bytes 786440 | tf_op jit(solution)/shard_map/ppermute | solution.py:10
  255.5 11.9 %collective-permute-start.17 = (f32[512,128]{1,0:T(8,128)S(1)}, f32[512,128]{1,0:T(8,128)S(1)}, u32[]{:S(2)}, u32[]{:S(2)}) collective-permute-start(f32[512,128]{1,0:T(8,128)S(1)} %slice_add_fusion.2), channel_id=1, source_target_pairs={{1,0},{2,1},{3,2},{4,3},{5,4},{6,5},{7,6},{8,7},{9,8},{10,9},{11,1... | collective-permute-start | bytes 786440 | tf_op jit(solution)/shard_map/ppermute | solution.py:10
  263.6 11.9 %collective-permute-start.13 = (f32[512,128]{1,0:T(8,128)S(1)}, f32[512,128]{1,0:T(8,128)S(1)}, u32[]{:S(2)}, u32[]{:S(2)}) collective-permute-start(f32[512,128]{1,0:T(8,128)S(1)} %slice_add_fusion.5), channel_id=1, source_target_pairs={{1,0},{2,1},{3,2},{4,3},{5,4},{6,5},{7,6},{8,7},{9,8},{10,9},{11,1... | collective-permute-start | bytes 786440 | tf_op jit(solution)/shard_map/ppermute | solution.py:10
  267.4 11.9 %collective-permute-start.18 = (f32[512,128]{1,0:T(8,128)S(1)}, f32[512,128]{1,0:T(8,128)S(1)}, u32[]{:S(2)}, u32[]{:S(2)}) collective-permute-start(f32[512,128]{1,0:T(8,128)S(1)} %slice_add_fusion.1), channel_id=1, source_target_pairs={{1,0},{2,1},{3,2},{4,3},{5,4},{6,5},{7,6},{8,7},{9,8},{10,9},{11,1... | collective-permute-start | bytes 786440 | tf_op jit(solution)/shard_map/ppermute | solution.py:10
  275.5 11.9 %collective-permute-start.14 = (f32[512,128]{1,0:T(8,128)S(1)}, f32[512,128]{1,0:T(8,128)S(1)}, u32[]{:S(2)}, u32[]{:S(2)}) collective-permute-start(f32[512,128]{1,0:T(8,128)S(1)} %slice_add_fusion.4), channel_id=1, source_target_pairs={{1,0},{2,1},{3,2},{4,3},{5,4},{6,5},{7,6},{8,7},{9,8},{10,9},{11,1... | collective-permute-start | bytes 786440 | tf_op jit(solution)/shard_map/ppermute | solution.py:10
  279.4 13.2 %collective-permute-start.19 = (f32[512,128]{1,0:T(8,128)S(1)}, f32[512,128]{1,0:T(8,128)S(1)}, u32[]{:S(2)}, u32[]{:S(2)}) collective-permute-start(f32[512,128]{1,0:T(8,128)S(1)} %slice_add_fusion), channel_id=1, source_target_pairs={{1,0},{2,1},{3,2},{4,3},{5,4},{6,5},{7,6},{8,7},{9,8},{10,9},{11,1... | collective-permute-start | bytes 786440 | tf_op jit(solution)/shard_map/ppermute | solution.py:10
  287.5 6.6 %collective-permute-start.15 = (f32[512,128]{1,0:T(8,128)S(1)}, f32[512,128]{1,0:T(8,128)}, u32[]{:S(2)}, u32[]{:S(2)}) collective-permute-start(f32[512,128]{1,0:T(8,128)S(1)} %slice_add_fusion.3), channel_id=1, source_target_pairs={{1,0},{2,1},{3,2},{4,3},{5,4},{6,5},{7,6},{8,7},{9,8},{10,9},{11,1... | collective-permute-start | bytes 786440 | tf_op jit(solution)/shard_map/ppermute | solution.py:10
  (41 other events, 128.2 us)
where the time goes:
time: 298 us; the launch traced here: 296 us
  matrix products  134 us (45%)
  starting transfers between devices  61.2 us (21%)
  local copies, waits for them, and re-layouts  46.2 us (16%)
  waiting for transfers between devices  41.1 us (14%)
  other arithmetic  11.6 us (4%)
    ppermute x20, starting transfers between devices, from_behind(): return lax.ppermute(block, axis, route)  61.2 us
    ppermute x20, waiting for transfers between devices, from_behind(): return lax.ppermute(block, axis, route)  41.1 us
    dot_general x8, matrix products, tile_step(): lax.dot_general(probs_low, cotangent, contract_rows, preferred_element_ty...  32.1 us
    dot_general x8, matrix products, tile_step(): jnp.dot(query_part, key_window.T, preferred_element_type=jnp.float32)  31.5 us
    dot_general x8, matrix products, tile_step(): jnp.dot(probs_low, value_window, preferred_element_type=jnp.float32)  29.7 us
    dot_general x8, matrix products, tile_step(): lax.dot_general(dscores, query_part, contract_rows, preferred_element_typ...  18.5 us
    while x80, local copies, waits for them, and re-layouts  14.5 us
    dynamic_slice x24, local copies, waits for them, and re-layouts, on_device(): lax.scan(tile_step, (zeros_window, zeros_window), (query_parts, cotangent...  14.1 us
  transfers between devices with their start and end apart: 20, of which 10 were waited for; matrix products, arithmetic and copies ran while one was open for 7% of the time, Pallas kernels for 0%

commit v1 on v0

v1 whole, which is shorter than its diff:
```python
import functools

import jax
import jax.numpy as jnp
from jax import lax
from jax.experimental import pallas as pl
from jax.experimental.pallas import tpu as pltpu
from jax.sharding import PartitionSpec as P

F32 = jnp.float32
BF16 = jnp.bfloat16
LOG2E = 1.4426950408889634
HIDE = 16384.0
NT = (((1,), (1,)), ((), ()))
BACK = 4


def dot(a, b):
    return jnp.dot(a, b, preferred_element_type=F32)


def dot_nt(a, b):
    return lax.dot_general(a, b, NT, preferred_element_type=F32)


def regions(hops, rows):
    half = rows // 2
    if hops == 0:
        return ((0, half, 0, half), (0, rows, half, half))
    if hops == BACK:
        return ((0, rows, 0, half), (half, half, half, half))
    return ((0, rows, 0, rows),)


def one_hot_rows(turn, width):
    row = lax.broadcasted_iota(jnp.int32, (width, turn.shape[1]), 0)
    high = jnp.where(row < 16, turn >> 4, -1)
    low = jnp.where((row >= 16) & (row < 32), (turn & 15) + 16, -1)
    return (row == high) | (row == low), row == 32


def kernel(
    inner_count,
    device_count,
    q_hbm,
    do_hbm,
    k_ref,
    v_ref,
    t_ref,
    sp_ref,
    gq_ref,
    gk_ref,
    gv_ref,
    q_s,
    do_s,
    kw,
    vw,
    ww,
    kc,
    kt,
    qc,
    es,
    ds,
    ms,
    ls,
    dl,
    gq_acc,
    gk_acc,
    gv_acc,
    gk_out,
    gv_out,
    gk_in,
    gv_in,
    in_sems,
    send_sems,
    recv_sems,
    gsend_sems,
    grecv_sems,
):
    rows, width = k_ref.shape
    heads = q_hbm.shape[1] // width
    scale = width ** (-0.5)
    to_exp2 = scale * LOG2E
    me = lax.axis_index("outer") * inner_count + lax.axis_index("inner")
    right = lax.rem(me + 1, device_count)
    left = lax.rem(me + device_count - 1, device_count)
    right_id = (right // inner_count, lax.rem(right, inner_count))
    left_id = (left // inner_count, lax.rem(left, inner_count))

    q_copy = pltpu.make_async_copy(q_hbm, q_s, in_sems.at[0])
    do_copy = pltpu.make_async_copy(do_hbm, do_s, in_sems.at[1])
    q_copy.start()
    do_copy.start()

    barrier = pltpu.get_barrier_semaphore()
    for neighbour in (left_id, right_id):
        pl.semaphore_signal(
            barrier, inc=1, device_id=neighbour, device_id_type=pl.DeviceIdType.MESH
        )

    turn = t_ref[...]
    pos = me * rows + lax.broadcasted_iota(jnp.int32, (1, rows), 1)
    inside = (pos >= sp_ref[:, 0:1]) & (pos < sp_ref[:, 1:2])
    tool = jnp.max(jnp.where(inside, 1.0, 0.0), axis=0, keepdims=True)
    ww[0] = jnp.where(tool > 0.5, turn, -1)

    pl.semaphore_wait(barrier, 2)

    def hop_copies(hop):
        parts = (
            (k_ref if hop == 1 else kw.at[hop - 2], kw.at[hop - 1]),
            (ww.at[hop - 1], ww.at[hop]),
            (v_ref if hop == 1 else vw.at[hop - 2], vw.at[hop - 1]),
        )
        return [
            pltpu.make_async_remote_copy(
                src_ref=src,
                dst_ref=dst,
                send_sem=send_sems.at[hop - 1, at],
                recv_sem=recv_sems.at[hop - 1, at],
                device_id=right_id,
                device_id_type=pl.DeviceIdType.MESH,
            )
            for at, (src, dst) in enumerate(parts)
        ]

    copies = {hop: hop_copies(hop) for hop in range(1, BACK + 1)}
    for copy in copies[1]:
        copy.start()

    def key_block(hops):
        return k_ref if hops == 0 else kw.at[hops - 1]

    def value_block(hops):
        return v_ref if hops == 0 else vw.at[hops - 1]

    hit, one = one_hot_rows(turn, width)
    qc[...] = jnp.transpose(jnp.where(hit | one, 1.0, 0.0)).astype(BF16)

    def prepare(hops):
        w = ww[hops]
        if hops:
            w = jnp.where(me >= hops, w, 1024)
        hit, one = one_hot_rows(w, width)
        code = jnp.where(hit, HIDE, jnp.where(one, -2.0 * HIDE, 0.0))
        code = jnp.where(w >= 0, code, 0.0)
        kc[hops] = jnp.transpose(code).astype(BF16)
        kt[hops] = jnp.transpose(key_block(hops)[...].astype(F32)).astype(BF16)

    def score_part(hops, h, part):
        k0, kn, r0, rn = part
        cols = pl.ds(pl.multiple_of(h * width, width), width)
        k_rows, q_rows = pl.ds(k0, kn), pl.ds(r0, rn)
        keyed = jnp.concatenate([key_block(hops)[k_rows, :], kc[hops, k_rows, :]], axis=1)
        asked = jnp.concatenate([q_s[q_rows, cols], qc[q_rows, :]], axis=1)
        s = dot_nt(keyed, asked)
        dp = dot_nt(value_block(hops)[k_rows, :], do_s[q_rows, cols])
        if hops in (0, BACK):
            key_at = k0 + lax.broadcasted_iota(jnp.int32, (kn, rn), 0)
            row_at = r0 + lax.broadcasted_iota(jnp.int32, (kn, rn), 1)
            seen = key_at <= row_at if hops == 0 else key_at > row_at
            s = jnp.where(seen, s, -2.0 * HIDE)
        top = jnp.max(s, axis=0, keepdims=True) * to_exp2
        if hops:
            before = ms[hops - 1, h, :, q_rows]
            top = jnp.maximum(before, top)
        e = jnp.exp2(s * to_exp2 - top)
        total = jnp.sum(e, axis=0, keepdims=True)
        inner = jnp.sum(e * dp, axis=0, keepdims=True)
        if hops:
            fade = jnp.exp2(before - top)
            total = total + ls[h, :, q_rows] * fade
            inner = inner + dl[h, :, q_rows] * fade
        ms[hops, h, :, q_rows] = top
        ls[h, :, q_rows] = total
        dl[h, :, q_rows] = inner
        es[hops, h, k_rows, q_rows] = e.astype(BF16)
        ds[hops, h, k_rows, q_rows] = dp.astype(BF16)

    def over_heads(step, unroll):
        def body(i, carry):
            for u in range(unroll):
                step(i * unroll + u)
            return carry

        lax.fori_loop(0, heads // unroll, body, 0)

    def score_block(hops):
        def step(h):
            for part in regions(hops, rows):
                score_part(hops, h, part)

        over_heads(step, 2)

    prepare(0)
    q_copy.wait()
    do_copy.wait()
    score_block(0)
    for hops in range(1, BACK + 1):
        for copy in copies[hops]:
            copy.wait_recv()
        if hops < BACK:
            for copy in copies[hops + 1]:
                copy.start()
        prepare(hops)
        score_block(hops)

    def finish(h):
        share = 1.0 / ls[h]
        last = ms[BACK, h]
        dl[h] = dl[h] * share
        for hops in range(BACK + 1):
            ms[hops, h] = jnp.exp2(ms[hops, h] - last) * share

    over_heads(finish, 1)

    def grad_part(hops, h, part):
        k0, kn, r0, rn = part
        cols = pl.ds(pl.multiple_of(h * width, width), width)
        k_rows, q_rows = pl.ds(k0, kn), pl.ds(r0, rn)
        p = es[hops, h, k_rows, q_rows].astype(F32) * ms[hops, h, :, q_rows]
        g = p * (ds[hops, h, k_rows, q_rows].astype(F32) - dl[h, :, q_rows])
        p = p.astype(BF16)
        g = g.astype(BF16)
        gk_acc[k_rows, :] += dot(g, q_s[q_rows, cols])
        gv_acc[k_rows, :] += dot(p, do_s[q_rows, cols])
        gq = dot(kt[hops, :, k_rows], g)
        if hops == BACK:
            gq_acc[h, :, q_rows] = gq
        else:
            gq_acc[h, :, q_rows] += gq

    def grad_copies(step):
        return [
            pltpu.make_async_remote_copy(
                src_ref=src.at[step],
                dst_ref=dst.at[step],
                send_sem=gsend_sems.at[step, at],
                recv_sem=grecv_sems.at[step, at],
                device_id=left_id,
                device_id_type=pl.DeviceIdType.MESH,
            )
            for at, (src, dst) in enumerate(((gk_out, gk_in), (gv_out, gv_in)))
        ]

    returns = [grad_copies(step) for step in range(BACK)]

    for step in range(BACK + 1):
        hops = BACK - step
        gk_acc[...] = jnp.zeros_like(gk_acc)
        gv_acc[...] = jnp.zeros_like(gv_acc)

        def grad_step(h):
            for part in regions(hops, rows):
                grad_part(hops, h, part)

        over_heads(grad_step, 2)
        if hops == 0:
            for h in range(heads):
                gq_ref[:, h * width : (h + 1) * width] = (
                    jnp.transpose(gq_acc[h] * scale)
                ).astype(BF16)
        gk = gk_acc[...]
        gv = gv_acc[...]
        if step:
            for copy in returns[step - 1]:
                copy.wait_recv()
            gk = gk + gk_in[step - 1].astype(F32)
            gv = gv + gv_in[step - 1].astype(F32)
        if hops:
            gk_out[step] = gk.astype(BF16)
            gv_out[step] = gv.astype(BF16)
            for copy in returns[step]:
                copy.start()
        else:
            gk_ref[...] = (gk * scale).astype(BF16)
            gv_ref[...] = gv.astype(BF16)

    for hop in range(1, BACK + 1):
        for copy in copies[hop]:
            copy.wait_send()
    for step in range(BACK):
        for copy in returns[step]:
            copy.wait_send()


def on_device(inner_count, device_count, queries, keys, values, grad_out, turn_ids, tool_spans):
    rows, width = keys.shape
    heads = queries.shape[1] // width
    vmem = pl.BlockSpec(memory_space=pltpu.VMEM)
    hbm = pl.BlockSpec(memory_space=pl.ANY)
    block = (rows, width)
    dma = pltpu.SemaphoreType.DMA
    flops = 2 * 5 * heads * rows * (BACK + 1) * rows * width
    return pl.pallas_call(
        functools.partial(kernel, inner_count, device_count),
        out_shape=(
            jax.ShapeDtypeStruct(queries.shape, BF16),
            jax.ShapeDtypeStruct(keys.shape, BF16),
            jax.ShapeDtypeStruct(values.shape, BF16),
        ),
        in_specs=[hbm, hbm, vmem, vmem, vmem, vmem],
        out_specs=(vmem, vmem, vmem),
        scratch_shapes=[
            pltpu.VMEM(queries.shape, BF16),
            pltpu.VMEM(queries.shape, BF16),
            pltpu.VMEM((BACK,) + block, BF16),
            pltpu.VMEM((BACK,) + block, BF16),
            pltpu.VMEM((BACK + 1, 1, rows), jnp.int32),
            pltpu.VMEM((BACK + 1,) + block, BF16),
            pltpu.VMEM((BACK + 1, width, rows), BF16),
            pltpu.VMEM(block, BF16),
            pltpu.VMEM((BACK + 1, heads, rows, rows), BF16),
            pltpu.VMEM((BACK + 1, heads, rows, rows), BF16),
            pltpu.VMEM((BACK + 1, heads, 1, rows), F32),
            pltpu.VMEM((heads, 1, rows), F32),
            pltpu.VMEM((heads, 1, rows), F32),
            pltpu.VMEM((heads, width, rows), F32),
            pltpu.VMEM(block, F32),
            pltpu.VMEM(block, F32),
            pltpu.VMEM((BACK,) + block, BF16),
            pltpu.VMEM((BACK,) + block, BF16),
            pltpu.VMEM((BACK,) + block, BF16),
            pltpu.VMEM((BACK,) + block, BF16),
            dma((2,)),
            dma((BACK, 3)),
            dma((BACK, 3)),
            dma((BACK, 2)),
            dma((BACK, 2)),
        ],
        compiler_params=pltpu.CompilerParams(
            collective_id=0, has_side_effects=True, vmem_limit_bytes=60 * 1024 * 1024
        ),
        cost_estimate=pl.CostEstimate(
            flops=flops, bytes_accessed=8 * 1024 * 1024, transcendentals=0
        ),
    )(queries, grad_out, keys, values, turn_ids.reshape(1, rows), tool_spans)


def solution(mesh):
    placed = (
        P(("outer", "inner"), None),
        P(("outer", "inner"), None),
        P(("outer", "inner"), None),
        P(("outer", "inner"), None),
        P(("outer", "inner")),
        P(),
    )
    return jax.shard_map(
        functools.partial(on_device, mesh.shape["inner"], mesh.size),
        mesh=mesh,
        in_specs=placed,
        out_specs=(
            P(("outer", "inner"), None),
            P(("outer", "inner"), None),
            P(("outer", "inner"), None),
        ),
        check_vma=False,
    )
```

time: 298 us -> 57.8 us (0.19)
  the two profiles are of different devices: /device:TPU:6 before, /device:TPU:1 now
where the time goes in v1:
time: 57.8 us; the launch traced here: 57.6 us
  Pallas kernels  51.6 us (89%)
  local copies, waits for them, and re-layouts  5.32 us (9%)
  between operations  0.66 us (1%)
    pallas_call x1, Pallas kernels, on_device(): pl.pallas_call(functools.partial(kernel, inner_count, device_count), out_...  51.6 us
    unnamed x10, local copies, waits for them, and re-layouts  5.32 us

profile of v1, /device:TPU:1, one launch (start us, length us, event | category | flops | bytes accessed | tf_op | source)
XLA Modules:
  0.0 57.6 jit_solution(12123504011241660361)
XLA Ops:
  0.6 0.0 copy-start.2
  0.6 0.7 %copy-done.2 = s32[128,2]{0,1:T(2,128)S(1)} copy-done((s32[128,2]{0,1:T(2,128)S(1)}, s32[128,2]{0,1:T(2,128)}, u32[]{:S(2)}) %copy-start.2) | copy-done | bytes 1048
  1.3 0.7 %copy.9.sp_ref = s32[128,2]{1,0:T(8,128)} copy(s32[128,2]{0,1:T(2,128)S(1)} %copy-done.2) | data formatting | bytes 2048 | tf_op args[5]
  2.1 51.6 %shard_map.85 = (bf16[512,1024]{1,0:T(8,128)(2,1)}, bf16[512,128]{1,0:T(8,128)(2,1)}, bf16[512,128]{1,0:T(8,128)(2,1)}) custom-call(bf16[512,1024]{1,0:T(8,128)(2,1)} %q_hbm.1, bf16[512,1024]{1,0:T(8,128)(2,1)} %do_hbm.1, bf16[512,128]{1,0:T(8,128)(2,1)} %k_ref.1, bf16[512,128]{1,0:T(8,128)(2,1)} %v_ref.1, s32[1,512]{1,0:T(1,128)} %bitcast.1, ...), custom_call_target="tpu_custom_call" | custom-call | flops 13421772800 | bytes 8388608 | tf_op jit(solution)/shard_map/pallas_call | solution.py:295
  53.7 0.0 copy-start.1
  53.7 2.3 %copy.13 = bf16[512,1024]{1,0:T(8,128)(2,1)} copy(bf16[512,1024]{1,0:T(8,128)(2,1)} %get-tuple-element.6) | data formatting | bytes 2097152
  56.0 0.0 copy-done.1
  56.0 0.0 copy-start
  56.0 0.7 %copy.14 = bf16[512,128]{1,0:T(8,128)(2,1)} copy(bf16[512,128]{1,0:T(8,128)(2,1)S(1)} %copy-done.1) | data formatting | bytes 262144
  56.7 0.3 copy-done
  57.0 0.7 %copy.15 = bf16[512,128]{1,0:T(8,128)(2,1)} copy(bf16[512,128]{1,0:T(8,128)(2,1)S(1)} %copy-done) | data formatting | bytes 262144
Async XLA Ops:
  0.6 0.7 %copy-start.2 = (s32[128,2]{0,1:T(2,128)S(1)}, s32[128,2]{0,1:T(2,128)}, u32[]{:S(2)}) copy-start(s32[128,2]{0,1:T(2,128)} %param.11) | copy-start | bytes 3076
  53.7 2.3 %copy-start.1 = (bf16[512,128]{1,0:T(8,128)(2,1)S(1)}, bf16[512,128]{1,0:T(8,128)(2,1)}, u32[]{:S(2)}) copy-start(bf16[512,128]{1,0:T(8,128)(2,1)} %get-tuple-element.7) | copy-start | bytes 393220
  56.0 1.0 %copy-start = (bf16[512,128]{1,0:T(8,128)(2,1)S(1)}, bf16[512,128]{1,0:T(8,128)(2,1)}, u32[]{:S(2)}) copy-start(bf16[512,128]{1,0:T(8,128)(2,1)} %get-tuple-element.8) | copy-start | bytes 393220

commit v2 on v1

--- a/solution.py
+++ b/solution.py
@@ -100,7 +100,10 @@
 
     turn = t_ref[...]
     pos = me * rows + lax.broadcasted_iota(jnp.int32, (1, rows), 1)
-    inside = (pos >= sp_ref[:, 0:1]) & (pos < sp_ref[:, 1:2])
+    count = sp_ref.shape[1]
+    first = jnp.transpose(jnp.broadcast_to(sp_ref[0:1, :], (8, count)))[:, 0:1]
+    after = jnp.transpose(jnp.broadcast_to(sp_ref[1:2, :], (8, count)))[:, 0:1]
+    inside = (pos >= first) & (pos < after)
     tool = jnp.max(jnp.where(inside, 1.0, 0.0), axis=0, keepdims=True)
     ww[0] = jnp.where(tool > 0.5, turn, -1)
 
@@ -190,7 +193,7 @@
             for part in regions(hops, rows):
                 score_part(hops, h, part)
 
-        over_heads(step, 2)
+        over_heads(step, 8)
 
     prepare(0)
     q_copy.wait()
@@ -254,7 +257,7 @@
             for part in regions(hops, rows):
                 grad_part(hops, h, part)
 
-        over_heads(grad_step, 2)
+        over_heads(grad_step, 4)
         if hops == 0:
             for h in range(heads):
                 gq_ref[:, h * width : (h + 1) * width] = (
@@ -284,6 +287,12 @@
             copy.wait_send()
 
 
+def hand_out(gq_in, gk_in, gv_in, gq_ref, gk_ref, gv_ref):
+    gq_ref[...] = gq_in[...]
+    gk_ref[...] = gk_in[...]
+    gv_ref[...] = gv_in[...]
+
+
 def on_device(inner_count, device_count, queries, keys, values, grad_out, turn_ids, tool_spans):
     rows, width = keys.shape
     heads = queries.shape[1] // width
@@ -292,7 +301,7 @@
     block = (rows, width)
     dma = pltpu.SemaphoreType.DMA
     flops = 2 * 5 * heads * rows * (BACK + 1) * rows * width
-    return pl.pallas_call(
+    parts = pl.pallas_call(
         functools.partial(kernel, inner_count, device_count),
         out_shape=(
             jax.ShapeDtypeStruct(queries.shape, BF16),
@@ -334,7 +343,14 @@
         cost_estimate=pl.CostEstimate(
             flops=flops, bytes_accessed=8 * 1024 * 1024, transcendentals=0
         ),
-    )(queries, grad_out, keys, values, turn_ids.reshape(1, rows), tool_spans)
+    )(queries, grad_out, keys, values, turn_ids.reshape(1, rows), tool_spans.T)
+    return pl.pallas_call(
+        hand_out,
+        out_shape=tuple(jax.ShapeDtypeStruct(part.shape, part.dtype) for part in parts),
+        in_specs=[vmem, vmem, vmem],
+        out_specs=(vmem, vmem, vmem),
+        scratch_shapes=[],
+    )(*parts)
 
 
 def solution(mesh):

time: 57.8 us -> 52 us (0.90)
  local copies, waits for them, and re-layouts: 5.32 us -> 0 us
    unnamed x10 -> x0, local copies, waits for them, and re-layouts: 5.32 us -> none
    pallas_call x1, Pallas kernels: 51.6 us -> 48.9 us  [on_device(): pl.pallas_call(functools.partial(kernel, inner_count, device_count), out_...]
    pallas_call x0 -> x1, Pallas kernels: none -> 2.38 us  [on_device(): pl.pallas_call(hand_out, out_shape=tuple((jax.ShapeDtypeStruct(part.shape...]
where the time goes in v2:
time: 52 us; the launch traced here: 51.9 us
  Pallas kernels  51.2 us (98%)
  between operations  0.64 us (1%)
    pallas_call x1, Pallas kernels, on_device(): pl.pallas_call(functools.partial(kernel, inner_count, device_count), out_...  48.9 us
    pallas_call x1, Pallas kernels, on_device(): pl.pallas_call(hand_out, out_shape=tuple((jax.ShapeDtypeStruct(part.shape...  2.38 us

profile of v2, /device:TPU:1, one launch (start us, length us, event | category | flops | bytes accessed | tf_op | source)
XLA Modules:
  0.0 51.9 jit_solution(6203471001352548368)
XLA Ops:
  0.6 48.9 %shard_map.85 = (bf16[512,1024]{1,0:T(8,128)(2,1)}, bf16[512,128]{1,0:T(8,128)(2,1)}, bf16[512,128]{1,0:T(8,128)(2,1)}) custom-call(bf16[512,1024]{1,0:T(8,128)(2,1)} %q_hbm.1, bf16[512,1024]{1,0:T(8,128)(2,1)} %do_hbm.1, bf16[512,128]{1,0:T(8,128)(2,1)} %k_ref.1, bf16[512,128]{1,0:T(8,128)(2,1)} %v_ref.1, s32[1,512]{1,0:T(1,128)} %bitcast.2, s32[2,128]{1,0:T(2,128)} %bitcast.3), custom_call_target="tpu_custom_call" | custom-call | flops 13421772800 | bytes 8388608 | tf_op jit(solution)/shard_map/pallas_call | solution.py:304
  49.5 2.4 %shard_map.86 = (bf16[512,1024]{1,0:T(8,128)(2,1)}, bf16[512,128]{1,0:T(8,128)(2,1)}, bf16[512,128]{1,0:T(8,128)(2,1)}) custom-call(bf16[512,1024]{1,0:T(8,128)(2,1)} %get-tuple-element.6.gq_in, bf16[512,128]{1,0:T(8,128)(2,1)} %get-tuple-element.7.gk_in, bf16[512,128]{1,0:T(8,128)(2,1)} %get-tuple-element.8.gv_in), custom_call_target="tpu_custom_call" | custom-call | tf_op jit(solution)/shard_map/pallas_call | solution.py:347

commit v3 on v2

--- a/solution.py
+++ b/solution.py
@@ -98,15 +98,6 @@
             barrier, inc=1, device_id=neighbour, device_id_type=pl.DeviceIdType.MESH
         )
 
-    turn = t_ref[...]
-    pos = me * rows + lax.broadcasted_iota(jnp.int32, (1, rows), 1)
-    count = sp_ref.shape[1]
-    first = jnp.transpose(jnp.broadcast_to(sp_ref[0:1, :], (8, count)))[:, 0:1]
-    after = jnp.transpose(jnp.broadcast_to(sp_ref[1:2, :], (8, count)))[:, 0:1]
-    inside = (pos >= first) & (pos < after)
-    tool = jnp.max(jnp.where(inside, 1.0, 0.0), axis=0, keepdims=True)
-    ww[0] = jnp.where(tool > 0.5, turn, -1)
-
     pl.semaphore_wait(barrier, 2)
 
     def hop_copies(hop):
@@ -128,8 +119,19 @@
         ]
 
     copies = {hop: hop_copies(hop) for hop in range(1, BACK + 1)}
-    for copy in copies[1]:
-        copy.start()
+    copies[1][0].start()
+    copies[1][2].start()
+
+    turn = t_ref[...]
+    pos = me * rows + lax.broadcasted_iota(jnp.int32, (1, rows), 1)
+    count = sp_ref.shape[1]
+    first = jnp.transpose(jnp.broadcast_to(sp_ref[0:1, :], (8, count)))[:, 0:1]
+    after = jnp.transpose(jnp.broadcast_to(sp_ref[1:2, :], (8, count)))[:, 0:1]
+    inside = (pos >= first) & (pos < after)
+    tool = jnp.max(jnp.where(inside, 1.0, 0.0), axis=0, keepdims=True)
+    ww[0] = jnp.where(tool > 0.5, turn, -1)
+
+    copies[1][1].start()
 
     def key_block(hops):
         return k_ref if hops == 0 else kw.at[hops - 1]
@@ -200,11 +202,10 @@
     do_copy.wait()
     score_block(0)
     for hops in range(1, BACK + 1):
-        for copy in copies[hops]:
+        for at, copy in enumerate(copies[hops]):
             copy.wait_recv()
-        if hops < BACK:
-            for copy in copies[hops + 1]:
-                copy.start()
+            if hops < BACK:
+                copies[hops + 1][at].start()
         prepare(hops)
         score_block(hops)
 
@@ -263,21 +264,17 @@
                 gq_ref[:, h * width : (h + 1) * width] = (
                     jnp.transpose(gq_acc[h] * scale)
                 ).astype(BF16)
-        gk = gk_acc[...]
-        gv = gv_acc[...]
-        if step:
-            for copy in returns[step - 1]:
-                copy.wait_recv()
-            gk = gk + gk_in[step - 1].astype(F32)
-            gv = gv + gv_in[step - 1].astype(F32)
-        if hops:
-            gk_out[step] = gk.astype(BF16)
-            gv_out[step] = gv.astype(BF16)
-            for copy in returns[step]:
-                copy.start()
-        else:
-            gk_ref[...] = (gk * scale).astype(BF16)
-            gv_ref[...] = gv.astype(BF16)
+        sums = ((gk_acc, gk_in, gk_out, gk_ref, scale), (gv_acc, gv_in, gv_out, gv_ref, 1.0))
+        for at, (acc, came, going, result, factor) in enumerate(sums):
+            total = acc[...]
+            if step:
+                returns[step - 1][at].wait_recv()
+                total = total + came[step - 1].astype(F32)
+            if hops:
+                going[step] = total.astype(BF16)
+                returns[step][at].start()
+            else:
+                result[...] = (total * factor).astype(BF16)
 
     for hop in range(1, BACK + 1):
         for copy in copies[hop]:

time: 52 us -> 51.6 us (level)
  no operation moved by 1% of the time
where the time goes in v3:
time: 51.6 us; the launch traced here: 51.5 us
  Pallas kernels  50.8 us (98%)
  between operations  0.64 us (1%)
    pallas_call x1, Pallas kernels, on_device(): pl.pallas_call(functools.partial(kernel, inner_count, device_count), out_...  48.5 us
    pallas_call x1, Pallas kernels, on_device(): pl.pallas_call(hand_out, out_shape=tuple((jax.ShapeDtypeStruct(part.shape...  2.38 us

profile of v3, /device:TPU:1, one launch (start us, length us, event | category | flops | bytes accessed | tf_op | source)
XLA Modules:
  0.0 51.5 jit_solution(17402267794376406894)
XLA Ops:
  0.6 48.5 %shard_map.85 = (bf16[512,1024]{1,0:T(8,128)(2,1)}, bf16[512,128]{1,0:T(8,128)(2,1)}, bf16[512,128]{1,0:T(8,128)(2,1)}) custom-call(bf16[512,1024]{1,0:T(8,128)(2,1)} %q_hbm.1, bf16[512,1024]{1,0:T(8,128)(2,1)} %do_hbm.1, bf16[512,128]{1,0:T(8,128)(2,1)} %k_ref.1, bf16[512,128]{1,0:T(8,128)(2,1)} %v_ref.1, s32[1,512]{1,0:T(1,128)} %bitcast.2, s32[2,128]{1,0:T(2,128)} %bitcast.3), custom_call_target="tpu_custom_call" | custom-call | flops 13421772800 | bytes 8388608 | tf_op jit(solution)/shard_map/pallas_call | solution.py:301
  49.1 2.4 %shard_map.86 = (bf16[512,1024]{1,0:T(8,128)(2,1)}, bf16[512,128]{1,0:T(8,128)(2,1)}, bf16[512,128]{1,0:T(8,128)(2,1)}) custom-call(bf16[512,1024]{1,0:T(8,128)(2,1)} %get-tuple-element.6.gq_in, bf16[512,128]{1,0:T(8,128)(2,1)} %get-tuple-element.7.gk_in, bf16[512,128]{1,0:T(8,128)(2,1)} %get-tuple-element.8.gv_in), custom_call_target="tpu_custom_call" | custom-call | tf_op jit(solution)/shard_map/pallas_call | solution.py:344
